TPU v7x, 32 devices: a whole 2x2x4 slice. The times are simulated.
32 devices in a mesh: groups: 1, cache: 16 (over z, y, x), dp: 2 (over core).
Axes of the slice: x: 2, y: 2, z: 4, core: 2. Of those that a mesh axis runs over, the one named last changes fastest.
Arguments:
- hidden: bfloat16 [640, 8192], P(('groups', 'dp'), 'cache'), may hold values from -6 to 6
- out_grad: bfloat16 [640, 8192], P(('groups', 'dp'), 'cache'), may hold values from -192 to 192
- norm_gain: float32 [8192], replicated, may hold values from 0.25 to 1.75
- w_query: bfloat16 [8192, 2048], P(None, 'cache'), may hold values from -0.0625 to 0.0625
- w_key: bfloat16 [8192, 8, 128], P(None, None, 'cache'), may hold values from -0.1875 to 0.1875
- w_value: bfloat16 [8192, 8, 128], P(None, None, 'cache'), may hold values from -0.0625 to 0.0625
- w_out: bfloat16 [2048, 8192], P('cache'), may hold values from -0.125 to 0.125
- cache_keys: float32 [1024, 1024], P(('groups', 'cache', 'dp')), may hold values from -512 to 512
- cache_values: float32 [1024, 1024], P(('groups', 'cache', 'dp')), may hold values from -6 to 6
- first_moment: float32 [2, 1024, 1024], P(None, ('groups', 'cache', 'dp')), may hold values from -0.1875 to 0.1875
- second_moment: float32 [2, 1024, 1024], P(None, ('groups', 'cache', 'dp')), may hold values from 0.0001 to 0.002
- conv_lengths: int32 [2, 4], P(('groups', 'dp')), may hold values from 1 to 160, 320 in all within a row
- row_offsets: int32 [2, 4], P(('groups', 'dp')), may hold values from 0 to 1023
Outputs:
- new_keys: float32 [1024, 1024], P(('groups', 'cache', 'dp'))
- new_values: float32 [1024, 1024], P(('groups', 'cache', 'dp'))
- new_first: float32 [2, 1024, 1024], P(None, ('groups', 'cache', 'dp'))
- new_second: float32 [2, 1024, 1024], P(None, ('groups', 'cache', 'dp'))
Inputs may be any that keep to these rules, and one draw needn't show every extreme that they name: `conv_lengths`: each dp index's 4 lengths sum to 320, and one of them is 160.
All inputs are finite; a program needn't handle non-finite values.
Results may differ from a plain program's by a relative error of at most 0.006.
The roundings to bfloat16 on the way count: a program that leaves them out, or rounds other values in their place, can miss the bound.
Values may be sent and summed in bfloat16 or wider, within the bound.
A program may use at most 128 MiB of HBM per device.

v0:
```python
import math
import jax
import jax.numpy as jnp
from jax import lax
from jax.sharding import PartitionSpec as P

KV = 8
ADAM_STEP = 10
THETA = 500000.0
BETA_ONE = 0.9
BETA_TWO = 0.999
RATE = 0.02
EPSILON = 1e-08


def rope_tables(position, head_width):
    half_width = head_width // 2
    inverse = jnp.exp(
        jnp.arange(half_width, dtype=jnp.float32) * (-2.0 * math.log(THETA) / head_width)
    )
    angles = position.astype(jnp.float32)[:, None] * inverse[None, :]
    return (jnp.cos(angles), jnp.sin(angles))


def rotate(tensor, cos_table, sin_table):
    half_width = tensor.shape[1] // 2
    first_half = tensor[:, :half_width]
    second_half = tensor[:, half_width:]
    return jnp.concatenate(
        [
            first_half * cos_table - second_half * sin_table,
            second_half * cos_table + first_half * sin_table,
        ],
        axis=1,
    )


def row_layout(lengths, offsets, row_count, cache_len):
    end_rows = jnp.cumsum(lengths)
    start_rows = end_rows - lengths
    row_index = jnp.arange(row_count, dtype=jnp.int32)
    segment = jnp.sum((row_index[:, None] >= end_rows[None, :]).astype(jnp.int32), axis=1)
    onehot = segment[:, None] == jnp.arange(lengths.shape[0], dtype=jnp.int32)[None, :]
    first_row = jnp.sum(jnp.where(onehot, start_rows[None, :], 0), axis=1)
    offset_row = jnp.sum(jnp.where(onehot, offsets[None, :], 0), axis=1)
    return (segment, cache_len + offset_row + row_index - first_row)


def attend(query, grad_out, cache_k, cache_v, self_k, self_v, allowed, score_scale):
    contract = (((1,), (1,)), ((), ()))
    score_cache = (
        lax.dot_general(query, cache_k, contract, preferred_element_type=jnp.float32) * score_scale
    )
    score_self = (
        lax.dot_general(query, self_k, contract, preferred_element_type=jnp.float32) * score_scale
    )
    score_self = jnp.where(allowed, score_self, -1e30)
    highest = jnp.maximum(
        jnp.max(score_cache, axis=1, keepdims=True), jnp.max(score_self, axis=1, keepdims=True)
    )
    exp_cache = jnp.exp(score_cache - highest)
    exp_self = jnp.exp(score_self - highest)
    denominator = jnp.sum(exp_cache, axis=1, keepdims=True) + jnp.sum(
        exp_self, axis=1, keepdims=True
    )
    prob_cache = exp_cache / denominator
    prob_self = exp_self / denominator
    weight_cache = prob_cache.astype(jnp.bfloat16)
    weight_self = prob_self.astype(jnp.bfloat16)
    attended = jnp.dot(weight_cache, cache_v, preferred_element_type=jnp.float32) + jnp.dot(
        weight_self, self_v, preferred_element_type=jnp.float32
    )
    delta_row = jnp.sum(grad_out.astype(jnp.float32) * attended, axis=1, keepdims=True)
    grad_prob = lax.dot_general(grad_out, cache_v, contract, preferred_element_type=jnp.float32)
    grad_score = (prob_cache * (grad_prob - delta_row)).astype(jnp.bfloat16)
    return (grad_score, weight_cache)


def adam_update(master, gradient, first, second):
    first_new = BETA_ONE * first + (1.0 - BETA_ONE) * gradient
    second_new = BETA_TWO * second + (1.0 - BETA_TWO) * gradient * gradient
    first_hat = first_new / (1.0 - BETA_ONE**ADAM_STEP)
    second_hat = second_new / (1.0 - BETA_TWO**ADAM_STEP)
    return (master - RATE * first_hat / (jnp.sqrt(second_hat) + EPSILON), first_new, second_new)


def source_total(pieces):
    head_width = pieces.shape[2]
    item_count = pieces.shape[1]
    summed = (
        pieces.astype(jnp.float32)
        .reshape(KV, pieces.shape[0] // KV, item_count, head_width)
        .sum(axis=1)
    )
    return summed.transpose(1, 0, 2).reshape(item_count, KV * head_width)


def totals_pair(pieces):
    return (source_total(pieces[0]), source_total(pieces[1]))


def per_device(
    hidden,
    out_grad,
    norm_gain,
    w_query,
    w_key,
    w_value,
    w_out,
    cache_keys,
    cache_values,
    first_moment,
    second_moment,
    conv_lengths,
    row_offsets,
):
    cache_count = lax.axis_size("cache")
    data_count = lax.axis_size("dp")
    pos_count = cache_keys.shape[0]
    device_count = cache_count * data_count
    cache_len = pos_count * device_count
    head_width = w_query.shape[1]
    column_share = w_key.shape[2]
    groups = cache_count // KV
    kv_head = lax.axis_index("cache") // groups
    score_scale = head_width ** (-0.5)
    hidden_full, grad_full = (
        lax.all_gather(hidden, "cache", axis=1, tiled=True),
        lax.all_gather(out_grad, "cache", axis=1, tiled=True),
    )
    row_count = hidden_full.shape[0]
    width_full = hidden_full.shape[1]
    hidden_f = hidden_full.astype(jnp.float32)
    inv_rms = lax.rsqrt(jnp.mean(hidden_f * hidden_f, axis=1, keepdims=True) + 1e-05)
    normed = (hidden_f * inv_rms * norm_gain).astype(jnp.bfloat16)
    segment, position = row_layout(conv_lengths[0], row_offsets[0], row_count, cache_len)
    cos_table, sin_table = rope_tables(position, head_width)
    query = rotate(
        jnp.dot(normed, w_query, preferred_element_type=jnp.float32), cos_table, sin_table
    ).astype(jnp.bfloat16)
    key_piece = (
        jnp.dot(
            normed, w_key.reshape(width_full, KV * column_share), preferred_element_type=jnp.float32
        )
        .astype(jnp.bfloat16)
        .reshape(row_count, KV, column_share)
    )
    value_piece = (
        jnp.dot(
            normed,
            w_value.reshape(width_full, KV * column_share),
            preferred_element_type=jnp.float32,
        )
        .astype(jnp.bfloat16)
        .reshape(row_count, KV, column_share)
    )
    keys_raw, values_self = (
        lax.all_gather(key_piece, "cache", axis=2, tiled=True),
        lax.all_gather(value_piece, "cache", axis=2, tiled=True),
    )
    own_keys = lax.dynamic_slice_in_dim(keys_raw, kv_head, 1, 1).reshape(row_count, head_width)
    self_k = rotate(own_keys.astype(jnp.float32), cos_table, sin_table).astype(jnp.bfloat16)
    self_v = lax.dynamic_slice_in_dim(values_self, kv_head, 1, 1).reshape(row_count, head_width)
    grad_out = lax.dot_general(
        grad_full, w_out, (((1,), (1,)), ((), ())), preferred_element_type=jnp.float32
    ).astype(jnp.bfloat16)
    cache_k = cache_keys.astype(jnp.bfloat16)
    cache_v = cache_values.astype(jnp.bfloat16)
    keys_all, values_all = (
        lax.all_gather(cache_k, ("cache", "dp"), axis=0, tiled=True),
        lax.all_gather(cache_v, ("cache", "dp"), axis=0, tiled=True),
    )
    head_k = lax.dynamic_slice_in_dim(keys_all, kv_head * head_width, head_width, 1)
    head_v = lax.dynamic_slice_in_dim(values_all, kv_head * head_width, head_width, 1)
    row_index = jnp.arange(row_count, dtype=jnp.int32)
    allowed = (segment[:, None] == segment[None, :]) & (row_index[None, :] <= row_index[:, None])
    grad_score, weight_cache = attend(
        query, grad_out, head_k, head_v, self_k, self_v, allowed, score_scale
    )
    transposed = (((0,), (0,)), ((), ()))
    key_part = (
        lax.dot_general(grad_score, query, transposed, preferred_element_type=jnp.float32)
        * score_scale
    ).astype(jnp.bfloat16)
    value_part = lax.dot_general(
        weight_cache, grad_out, transposed, preferred_element_type=jnp.float32
    ).astype(jnp.bfloat16)
    send_k = key_part.reshape(device_count, pos_count, head_width)
    send_v = value_part.reshape(device_count, pos_count, head_width)
    grad_k, grad_v = totals_pair(
        (
            lax.all_to_all(send_k, ("cache", "dp"), split_axis=0, concat_axis=0, tiled=True),
            lax.all_to_all(send_v, ("cache", "dp"), split_axis=0, concat_axis=0, tiled=True),
        )
    )
    gradient = jnp.stack([grad_k, grad_v])
    master = jnp.stack([cache_keys, cache_values])
    new_master, first_new, second_new = adam_update(master, gradient, first_moment, second_moment)
    return (new_master[0], new_master[1], first_new, second_new)


def solution(mesh):
    return jax.shard_map(
        per_device,
        mesh=mesh,
        in_specs=(
            P(("groups", "dp"), "cache"),
            P(("groups", "dp"), "cache"),
            P(),
            P(None, "cache"),
            P(None, None, "cache"),
            P(None, None, "cache"),
            P("cache", None),
            P(("groups", "cache", "dp"), None),
            P(("groups", "cache", "dp"), None),
            P(None, ("groups", "cache", "dp"), None),
            P(None, ("groups", "cache", "dp"), None),
            P(("groups", "dp"), None),
            P(("groups", "dp"), None),
        ),
        out_specs=(
            P(("groups", "cache", "dp"), None),
            P(("groups", "cache", "dp"), None),
            P(None, ("groups", "cache", "dp"), None),
            P(None, ("groups", "cache", "dp"), None),
        ),
        check_vma=False,
    )
```

profile of v0, /device:TPU:0, one launch (start us, length us, event | category | flops | bytes accessed | tf_op | source)
XLA Modules:
  0.0 358.8 jit_solution(13640633634136398060)
XLA Ops:
  7.2 0.0 copy-start
  7.2 0.0 all-gather.5.cloned.1.call-start
  7.2 0.7 all-gather.5.cloned.1.call-update
  7.9 0.0 all-gather.7.cloned.1.call-start
  8.0 1.5 convert_element_type.63
  9.5 0.0 all-gather.7.cloned.1.call-update
  9.5 0.0 all-gather.9.cloned.1.call-start
  9.6 0.7 all-gather.9.cloned.1.call-update
  10.3 0.0 all-gather.11.cloned.1.call-start
  10.3 1.5 convert_element_type.68
  11.9 0.0 all-gather.11.cloned.1.call-update
  11.9 0.0 copy-start.11
  11.9 0.8 reduce-window.4
  12.8 0.7 fusion.54
  13.4 0.1 convert_reduce_fusion.2
  13.5 0.7 select_reduce_fusion.1
  14.3 90.2 %all-gather.5.cloned.1.call-done = bf16[320,8192]{1,0:T(8,128)(2,1)} async-done(((bf16[320,512]{1,0:T(8,128)(2,1)}), bf16[320,8192]{1,0:T(8,128)(2,1)}) %all-gather.5.cloned.1.call-update) | async-done | bytes 5242896 | tf_op jit(solution)/shard_map/all_gather | solution.py:128
  104.5 3.8 %fusion = f32[320]{0:T(512)S(1)} fusion(bf16[320,8192]{1,0:T(8,128)(2,1)} %all-gather.5.cloned.1.call-done), kind=kLoop, calls=%fused_computation.2 | loop fusion | flops 7864000 | bytes 5244160 | tf_op jit(solution)/shard_map/reduce_sum | solution.py:134
  108.2 0.0 copy-done.11
  108.3 0.3 copy-done.2
  108.5 1.6 fusion.2
  110.1 0.0 copy-done.3
  110.2 0.0 copy-start.1
  110.2 1.6 fusion.13
  111.8 0.7 copy-done.1
  112.5 43.7 %all_gather.20 = bf16[320,8,128]{0,1,2:T(8,128)(2,1)S(1)} all-gather(bf16[320,8,8]{0,1,2:T(8,128)(2,1)S(1)} %copy.24), channel_id=1, replica_groups=mesh['groups'=1,'cache'=16,'dp'=2] {'cache'}, dimensions={2}, use_global_device_ids=true | all-gather | bytes 696320 | tf_op jit(solution)/shard_map/all_gather | solution.py:158
  156.3 0.2 constant_dynamic-slice_fusion
  156.5 0.2 copy.28
  156.7 0.0 copy-done
  156.7 4.0 %fusion.59 = f32[320,128]{1,0:T(8,128)S(1)} fusion(bf16[320,8192]{1,0:T(8,128)(2,1)} %copy-done.1, bf16[8192,128]{1,0:T(8,128)(2,1)S(1)} %copy-done), kind=kOutput, calls=%fused_computation.93 | convolution fusion | flops 671088640 | bytes 7503872 | tf_op jit(solution)/shard_map/dot_general | solution.py:139
  160.7 0.7 fusion.41
  161.5 0.0 copy-start.5
  161.5 0.0 copy-start.6
  161.5 2.4 all-gather.7.cloned.1.call-done
  163.9 1.5 fusion.57
  165.4 0.4 fusion.58
  165.8 0.1 fusion.19
  165.9 0.4 fusion.10
  166.3 0.0 copy-done.5
  166.3 0.0 copy-done.6
  166.3 0.0 copy-done.4
  166.3 4.1 %fusion.14 = bf16[320,8,8]{0,2,1:T(8,128)(2,1)S(1)} fusion(bf16[320,8192]{1,0:T(8,128)(2,1)} %copy-done.1, bf16[8192,8,8]{0,2,1:T(8,128)(2,1)S(1)} %copy-done.4), kind=kOutput, calls=%fused_computation.25 | convolution fusion | flops 335564800 | bytes 6332416 | tf_op jit(solution)/shard_map/dot_general | solution.py:149
  170.5 48.7 %all_gather.23 = bf16[320,8,128]{0,2,1:T(8,128)(2,1)S(1)} all-gather(bf16[320,8,8]{0,2,1:T(8,128)(2,1)S(1)} %fusion.14), channel_id=1, replica_groups=mesh['groups'=1,'cache'=16,'dp'=2] {'cache'}, dimensions={2}, use_global_device_ids=true | all-gather | bytes 696320 | tf_op jit(solution)/shard_map/all_gather | solution.py:159
  219.2 0.9 fusion.24
  220.1 0.3 fusion.9
  220.4 40.8 %all-gather.9.cloned.1.call-done = bf16[320,8192]{1,0:T(8,128)(2,1)} async-done(((bf16[320,512]{1,0:T(8,128)(2,1)}), bf16[320,8192]{1,0:T(8,128)(2,1)}) %all-gather.9.cloned.1.call-update) | async-done | bytes 5242896 | tf_op jit(solution)/shard_map/all_gather | solution.py:129
  261.3 4.7 %convolution_convert_fusion.1 = bf16[320,128]{1,0:T(8,128)(2,1)S(1)} fusion(bf16[320,8192]{1,0:T(8,128)(2,1)} %all-gather.9.cloned.1.call-done, bf16[128,8192]{1,0:T(8,128)(2,1)} %param.19), kind=kOutput, calls=%fused_computation.20 | convolution fusion | flops 671129600 | bytes 7421952 | tf_op jit(solution)/shard_map/dot_general | solution.py:164
  265.9 53.2 %all-gather.11.cloned.1.call-done = bf16[1024,1024]{1,0:T(8,128)(2,1)} async-done(((bf16[32,1024]{1,0:T(8,128)(2,1)}), bf16[1024,1024]{1,0:T(8,128)(2,1)}) %all-gather.11.cloned.1.call-update) | async-done | bytes 2097168 | tf_op jit(solution)/shard_map/all_gather | solution.py:171
  319.1 1.4 fusion.12
  320.6 2.5 fusion.8
  323.0 3.6 all-to-all-start
  326.6 1.1 convolution_convert_fusion
  327.8 9.4 %all-to-all-done = bf16[32,32,128]{2,1,0:T(8,128)(2,1)} async-done(((bf16[32,32,128]{2,1,0:T(8,128)(2,1)}), bf16[32,32,128]{2,1,0:T(8,128)(2,1)}, u32[]{:S(2)}, u32[]{:S(2)}) %all-to-all-start) | async-done | bytes 262176 | tf_op jit(solution)/shard_map/all_to_all | solution.py:192
  337.2 2.6 all-to-all-start.1
  339.8 1.0 convert_reduce_fusion.1
  340.8 0.1 copy.26
  340.9 9.5 %all-to-all-done.1 = bf16[32,32,128]{2,1,0:T(8,128)(2,1)S(1)} async-done(((bf16[32,32,128]{2,1,0:T(8,128)(2,1)}), bf16[32,32,128]{2,1,0:T(8,128)(2,1)S(1)}, u32[]{:S(2)}, u32[]{:S(2)}) %all-to-all-start.1) | async-done | bytes 262176 | tf_op jit(solution)/shard_map/all_to_all | solution.py:193
  350.4 0.1 copy.27
  350.6 0.0 copy-done.7
  350.6 0.0 copy-done.8
  350.6 0.0 copy-done.9
  350.6 0.0 copy-done.10
  350.6 1.0 maximum_subtract_fusion
  351.6 0.7 slice_bitcast_fusion
  (19 shorter events, 0.2 us)
Async XLA Ops:
  7.2 149.5 %copy-start = (bf16[8192,128]{1,0:T(8,128)(2,1)S(1)}, bf16[8192,128]{1,0:T(8,128)(2,1)}, u32[]{:S(2)}) copy-start(bf16[8192,128]{1,0:T(8,128)(2,1)} %param.16) | copy-start | bytes 6291460
  7.2 97.3 %all-gather.5.cloned.1.call-start = ((), (), s32[]{:S(2)}) async-start(), calls=%async_computation.2 | async-start | bytes 5570560 | tf_op jit(solution)/shard_map/all_gather | solution.py:128
  7.9 156.0 %all-gather.7.cloned.1.call-start = ((), (), s32[]{:S(2)}) async-start(), calls=%async_computation.3 | async-start | bytes 2162688 | tf_op jit(solution)/shard_map/all_gather | solution.py:170
  9.5 251.7 %all-gather.9.cloned.1.call-start = ((), (), s32[]{:S(2)}) async-start(), calls=%async_computation.4 | async-start | bytes 5570560 | tf_op jit(solution)/shard_map/all_gather | solution.py:129
  10.3 308.9 %all-gather.11.cloned.1.call-start = ((), (), s32[]{:S(2)}) async-start(), calls=%async_computation.5 | async-start | bytes 2162688 | tf_op jit(solution)/shard_map/all_gather | solution.py:171
  11.9 96.4 %copy-start.11 = (f32[8192]{0:T(1024)S(1)}, f32[8192]{0:T(1024)}, u32[]{:S(2)}) copy-start(f32[8192]{0:T(1024)} %param.15) | copy-start | bytes 98308
  104.5 4.0 %copy-start.2 = (bf16[320,8192]{1,0:T(8,128)(2,1)S(1)}, bf16[320,8192]{1,0:T(8,128)(2,1)}, u32[]{:S(2)}) copy-start(bf16[320,8192]{1,0:T(8,128)(2,1)} %all-gather.5.cloned.1.call-done) | copy-start | bytes 15728644
  108.5 1.6 copy-start.3
  110.2 2.3 copy-start.1
  161.5 4.8 %copy-start.5 = (bf16[320,64]{1,0:T(8,128)(2,1)}, bf16[320,64]{1,0:T(8,128)(2,1)S(1)}, u32[]{:S(2)}) copy-start(bf16[320,64]{1,0:T(8,128)(2,1)S(1)} %get-tuple-element.15) | copy-start | bytes 122884
  161.5 4.8 %copy-start.6 = (bf16[320,64]{1,0:T(8,128)(2,1)}, bf16[320,64]{1,0:T(8,128)(2,1)S(1)}, u32[]{:S(2)}) copy-start(bf16[320,64]{1,0:T(8,128)(2,1)S(1)} %get-tuple-element.16) | copy-start | bytes 122884
  163.9 2.4 copy-start.4
  323.0 14.2 %all-to-all-start = ((bf16[32,32,128]{2,1,0:T(8,128)(2,1)}), bf16[32,32,128]{2,1,0:T(8,128)(2,1)}, u32[]{:S(2)}, u32[]{:S(2)}) async-start(bf16[32,32,128]{2,1,0:T(8,128)(2,1)} %bitcast.50), calls=%async_computation | async-start | bytes 524288 | tf_op jit(solution)/shard_map/all_to_all | solution.py:192
  327.7 22.8 %copy-start.7 = (f32[32,1024]{1,0:T(8,128)S(1)}, f32[32,1024]{1,0:T(8,128)}, u32[]{:S(2)}) copy-start(f32[32,1024]{1,0:T(8,128)} %param.21) | copy-start | bytes 393220
  327.7 22.8 %copy-start.8 = (f32[32,1024]{1,0:T(8,128)S(1)}, f32[32,1024]{1,0:T(8,128)}, u32[]{:S(2)}) copy-start(f32[32,1024]{1,0:T(8,128)} %param.20) | copy-start | bytes 393220
  327.7 22.8 %copy-start.9 = (f32[2,32,1024]{2,1,0:T(8,128)S(1)}, f32[2,32,1024]{2,1,0:T(8,128)}, u32[]{:S(2)}) copy-start(f32[2,32,1024]{2,1,0:T(8,128)} %param.22) | copy-start | bytes 786436
  327.7 22.9 %copy-start.10 = (f32[2,32,1024]{2,1,0:T(8,128)S(1)}, f32[2,32,1024]{2,1,0:T(8,128)}, u32[]{:S(2)}) copy-start(f32[2,32,1024]{2,1,0:T(8,128)} %param.23) | copy-start | bytes 786436
  337.2 13.2 %all-to-all-start.1 = ((bf16[32,32,128]{2,1,0:T(8,128)(2,1)}), bf16[32,32,128]{2,1,0:T(8,128)(2,1)S(1)}, u32[]{:S(2)}, u32[]{:S(2)}) async-start(bf16[32,32,128]{2,1,0:T(8,128)(2,1)} %bitcast.49), calls=%async_computation.1 | async-start | bytes 524288 | tf_op jit(solution)/shard_map/all_to_all | solution.py:193
Sparse Core Ops, SparseCore 0:
  10.7 93.6 all-gather.4
  107.9 55.9 all-gather.6
  166.7 94.5 all-gather.8
  264.6 54.5 all-gather.10
where the time goes:
time: 359 us
  waiting for transfers between devices  207 us (58%)
  blocking collectives  92.5 us (26%)
  matrix products  22.3 us (6%)
  other arithmetic  14.4 us (4%)
  between operations  14.1 us (4%)
  starting transfers between devices  6.33 us (2%)
    all_gather x1, waiting for transfers between devices, per_device(): lax.all_gather(hidden, 'cache', axis=1, tiled=True)  90.2 us
    all_gather x1, waiting for transfers between devices, per_device(): lax.all_gather(cache_v, ('cache', 'dp'), axis=0, tiled=True)  53.2 us
    all_gather x1, blocking collectives, per_device(): lax.all_gather(value_piece, 'cache', axis=2, tiled=True)  48.7 us
    all_gather x1, blocking collectives, per_device(): lax.all_gather(key_piece, 'cache', axis=2, tiled=True)  43.7 us
    all_gather x1, waiting for transfers between devices, per_device(): lax.all_gather(out_grad, 'cache', axis=1, tiled=True)  40.8 us
    all_to_all x1, waiting for transfers between devices, per_device(): lax.all_to_all(send_v, ('cache', 'dp'), split_axis=0, concat_axis=0, tile...  9.46 us
    all_to_all x1, waiting for transfers between devices, per_device(): lax.all_to_all(send_k, ('cache', 'dp'), split_axis=0, concat_axis=0, tile...  9.45 us
  transfers between devices with their start and end apart: 6, of which 6 were waited for; matrix products, arithmetic and copies ran while one was open for 9% of the time, Pallas kernels for 0%

commit v1 on v0

--- a/solution.py
+++ b/solution.py
@@ -11,6 +11,22 @@
 BETA_TWO = 0.999
 RATE = 0.02
 EPSILON = 1e-08
+
+
+def ring_gather(x, axis, dim):
+    ways, here, step = (lax.axis_size(axis), lax.axis_index(axis), x.shape[dim])
+    lengths = [n * ways if d == dim else n for d, n in enumerate(x.shape)]
+    full = lax.dynamic_update_slice_in_dim(jnp.zeros(lengths, x.dtype), x, here * step, axis=dim)
+    going_up = going_down = x
+    for far in range(1, ways // 2 + 1):
+        going_up = lax.ppermute(going_up, axis, [(d, (d + 1) % ways) for d in range(ways)])
+        full = lax.dynamic_update_slice_in_dim(full, going_up, (here - far) % ways * step, axis=dim)
+        if 2 * far < ways:
+            going_down = lax.ppermute(going_down, axis, [(d, (d - 1) % ways) for d in range(ways)])
+            full = lax.dynamic_update_slice_in_dim(
+                full, going_down, (here + far) % ways * step, axis=dim
+            )
+    return full
 
 
 def rope_tables(position, head_width):
@@ -156,7 +172,7 @@
     )
     keys_raw, values_self = (
         lax.all_gather(key_piece, "cache", axis=2, tiled=True),
-        lax.all_gather(value_piece, "cache", axis=2, tiled=True),
+        ring_gather(value_piece, "cache", 2),
     )
     own_keys = lax.dynamic_slice_in_dim(keys_raw, kv_head, 1, 1).reshape(row_count, head_width)
     self_k = rotate(own_keys.astype(jnp.float32), cos_table, sin_table).astype(jnp.bfloat16)

time: 359 us -> 398 us (1.11)
  blocking collectives: 92.5 us -> 43.2 us
  starting transfers between devices: 6.33 us -> 46.2 us
  waiting for transfers between devices: 207 us -> 246 us
  local copies, waits for them, and re-layouts: 2.34 us -> 13.6 us
    all_gather x1 -> x0, blocking collectives: 48.7 us -> none  [per_device(): lax.all_gather(value_piece, 'cache', axis=2, tiled=True)]
    all_gather x1, waiting for transfers between devices: 40.8 us -> 85.9 us  [per_device(): lax.all_gather(out_grad, 'cache', axis=1, tiled=True)]
    ppermute x0 -> x15, starting transfers between devices: none -> 39.8 us  [the longest x7 36.8 us: ring_gather(): lax.ppermute(going_down, axis, [(d, (d - 1) % ways) for d in range(ways)])]
    dynamic_update_slice x0 -> x15, local copies, waits for them, and re-layouts: none -> 11 us  [the longest x8 5.83 us: ring_gather(): lax.dynamic_update_slice_in_dim(full, going_up, (here - far) % ways * ste...]
    ppermute x0 -> x15, waiting for transfers between devices: none -> 10.2 us  [the longest x8 10.2 us: ring_gather(): lax.ppermute(going_up, axis, [(d, (d + 1) % ways) for d in range(ways)])]
    all_to_all x1, waiting for transfers between devices: 9.46 us -> 0.01 us  [per_device(): lax.all_to_all(send_v, ('cache', 'dp'), split_axis=0, concat_axis=0, tile...]
    all_gather x1, waiting for transfers between devices: 53.2 us -> 48.8 us  [per_device(): lax.all_gather(cache_v, ('cache', 'dp'), axis=0, tiled=True)]
  transfers between devices with their start and end apart: 6 -> 21, of which waited for: 6 -> 10; matrix products, arithmetic and copies ran while one was open for 9% -> 11% of each run, Pallas kernels for 0% -> 0%
where the time goes in v1:
time: 398 us; the launch traced here: 397 us
  waiting for transfers between devices  246 us (62%)
  starting transfers between devices  46.2 us (12%)
  blocking collectives  43.2 us (11%)
  matrix products  20 us (5%)
  between operations  14.5 us (4%)
  other arithmetic  14.4 us (4%)
  local copies, waits for them, and re-layouts  13.6 us (3%)
    all_gather x1, waiting for transfers between devices, per_device(): lax.all_gather(hidden, 'cache', axis=1, tiled=True)  89.9 us
    all_gather x1, waiting for transfers between devices, per_device(): lax.all_gather(out_grad, 'cache', axis=1, tiled=True)  85.9 us
    all_gather x1, waiting for transfers between devices, per_device(): lax.all_gather(cache_v, ('cache', 'dp'), axis=0, tiled=True)  48.8 us
    all_gather x1, blocking collectives, per_device(): lax.all_gather(key_piece, 'cache', axis=2, tiled=True)  43.2 us
    ppermute x7, starting transfers between devices, ring_gather(): lax.ppermute(going_down, axis, [(d, (d - 1) % ways) for d in range(ways)])  36.8 us
    ppermute x8, waiting for transfers between devices, ring_gather(): lax.ppermute(going_up, axis, [(d, (d + 1) % ways) for d in range(ways)])  10.2 us
    all_to_all x1, waiting for transfers between devices, per_device(): lax.all_to_all(send_k, ('cache', 'dp'), split_axis=0, concat_axis=0, tile...  9.47 us
  transfers between devices with their start and end apart: 21, of which 10 were waited for; matrix products, arithmetic and copies ran while one was open for 11% of the time, Pallas kernels for 0%

profile of v1, /device:TPU:0, one launch (start us, length us, event | category | flops | bytes accessed | tf_op | source)
XLA Modules:
  0.0 397.4 jit_solution(6505183119209014575)
XLA Ops:
  7.2 0.7 all-gather.5.cloned.1.call-update
  8.0 1.5 convert_element_type.63
  9.6 0.7 all-gather.9.cloned.1.call-update
  10.3 1.5 convert_element_type.68
  12.2 0.8 reduce-window.4
  13.0 0.7 fusion.54
  13.9 0.7 select_reduce_fusion.1
  14.6 89.9 %all-gather.5.cloned.1.call-done = bf16[320,8192]{1,0:T(8,128)(2,1)} async-done(((bf16[320,512]{1,0:T(8,128)(2,1)}), bf16[320,8192]{1,0:T(8,128)(2,1)}) %all-gather.5.cloned.1.call-update) | async-done | bytes 5242896 | tf_op jit(solution)/shard_map/all_gather | solution.py:144
  104.5 3.8 fusion
  108.3 0.3 copy-done.2
  108.5 1.6 fusion.2
  110.3 1.7 constant_dynamic-update-slice_fusion.17
  111.9 1.5 collective-permute-start
  113.4 4.2 %collective-permute-start.1 = (bf16[320,8,8]{0,2,1:T(8,128)(2,1)S(1)}, bf16[320,8,8]{0,2,1:T(8,128)(2,1)}, u32[]{:S(2)}, u32[]{:S(2)}) collective-permute-start(bf16[320,8,8]{0,2,1:T(8,128)(2,1)S(1)} %get-tuple-element.22), channel_id=1, source_target_pairs={{0,30},{2,0},{4,2},{6,4},{8,6},{10,8},{12,10},{14,12},{16,14},{18,... | collective-permute-start | bytes 122888 | tf_op jit(solution)/shard_map/ppermute | solution.py:25
  117.6 1.6 fusion.13
  119.3 43.2 %all_gather.17 = bf16[320,8,128]{0,1,2:T(8,128)(2,1)S(1)} all-gather(bf16[320,8,8]{0,1,2:T(8,128)(2,1)S(1)} %copy.24), channel_id=1, replica_groups=mesh['groups'=1,'cache'=16,'dp'=2] {'cache'}, dimensions={2}, use_global_device_ids=true | all-gather | bytes 696320 | tf_op jit(solution)/shard_map/all_gather | solution.py:174
  162.9 4.0 %fusion.59 = f32[320,128]{1,0:T(8,128)S(1)} fusion(bf16[320,8192]{1,0:T(8,128)(2,1)} %copy-done.1, bf16[8192,128]{1,0:T(8,128)(2,1)S(1)} %copy-done), kind=kOutput, calls=%fused_computation.109 | convolution fusion | flops 671088640 | bytes 7503872 | tf_op jit(solution)/shard_map/dot_general | solution.py:155
  166.9 0.7 fusion.41
  167.7 1.4 fusion.57
  169.2 0.4 fusion.58
  169.5 0.8 copy-done.10
  170.4 0.4 fusion.10
  170.8 0.3 fusion.9
  171.1 85.9 %all-gather.9.cloned.1.call-done = bf16[320,8192]{1,0:T(8,128)(2,1)} async-done(((bf16[320,512]{1,0:T(8,128)(2,1)}), bf16[320,8192]{1,0:T(8,128)(2,1)}) %all-gather.9.cloned.1.call-update) | async-done | bytes 5242896 | tf_op jit(solution)/shard_map/all_gather | solution.py:145
  257.1 4.7 %convolution_convert_fusion.1 = bf16[320,128]{1,0:T(8,128)(2,1)S(1)} fusion(bf16[320,8192]{1,0:T(8,128)(2,1)} %all-gather.9.cloned.1.call-done, bf16[128,8192]{1,0:T(8,128)(2,1)} %param.19), kind=kOutput, calls=%fused_computation.20 | convolution fusion | flops 671129600 | bytes 7421952 | tf_op jit(solution)/shard_map/dot_general | solution.py:180
  261.7 1.1 convolution_convert_fusion
  262.8 3.5 all-to-all-start.1
  266.3 48.8 %all-gather.11.cloned.1.call-done = bf16[1024,1024]{1,0:T(8,128)(2,1)} async-done(((bf16[32,1024]{1,0:T(8,128)(2,1)}), bf16[1024,1024]{1,0:T(8,128)(2,1)}) %all-gather.11.cloned.1.call-update) | async-done | bytes 2097168 | tf_op jit(solution)/shard_map/all_gather | solution.py:187
  315.2 1.3 fusion.21
  316.5 1.5 collective-permute-start.2
  318.0 4.2 %collective-permute-start.3 = (bf16[320,8,8]{0,2,1:T(8,128)(2,1)}, bf16[320,8,8]{0,2,1:T(8,128)(2,1)S(1)}, u32[]{:S(2)}, u32[]{:S(2)}) collective-permute-start(bf16[320,8,8]{0,2,1:T(8,128)(2,1)} %collective-permute-done.1), channel_id=1, source_target_pairs={{0,30},{2,0},{4,2},{6,4},{8,6},{10,8},{12,10},{14,12},{16,14},{18,... | collective-permute-start | bytes 122888 | tf_op jit(solution)/shard_map/ppermute | solution.py:25
  322.2 1.4 constant_dynamic-update-slice_fusion.16
  323.6 1.4 constant_dynamic-update-slice_fusion.15
  325.1 5.6 %collective-permute-start.5 = (bf16[320,8,8]{0,2,1:T(8,128)(2,1)S(1)}, bf16[320,8,8]{0,2,1:T(8,128)(2,1)S(1)}, u32[]{:S(2)}, u32[]{:S(2)}) collective-permute-start(bf16[320,8,8]{0,2,1:T(8,128)(2,1)S(1)} %collective-permute-done.3), channel_id=1, source_target_pairs={{0,30},{2,0},{4,2},{6,4},{8,6},{10,8},{12,10},{14,12},{16,14},{18,... | collective-permute-start | bytes 122888 | tf_op jit(solution)/shard_map/ppermute | solution.py:25
  330.7 0.6 constant_dynamic-update-slice_fusion.14
  331.3 0.6 constant_dynamic-update-slice_fusion.13
  332.0 0.8 collective-permute-done.4
  332.8 5.7 %collective-permute-start.7 = (bf16[320,8,8]{0,2,1:T(8,128)(2,1)S(1)}, bf16[320,8,8]{0,2,1:T(8,128)(2,1)S(1)}, u32[]{:S(2)}, u32[]{:S(2)}) collective-permute-start(bf16[320,8,8]{0,2,1:T(8,128)(2,1)S(1)} %collective-permute-done.5), channel_id=1, source_target_pairs={{0,30},{2,0},{4,2},{6,4},{8,6},{10,8},{12,10},{14,12},{16,14},{18,... | collective-permute-start | bytes 122888 | tf_op jit(solution)/shard_map/ppermute | solution.py:25
  338.5 0.6 constant_dynamic-update-slice_fusion.12
  339.1 0.6 constant_dynamic-update-slice_fusion.11
  339.7 0.8 collective-permute-done.6
  340.5 5.6 %collective-permute-start.9 = (bf16[320,8,8]{0,2,1:T(8,128)(2,1)S(1)}, bf16[320,8,8]{0,2,1:T(8,128)(2,1)S(1)}, u32[]{:S(2)}, u32[]{:S(2)}) collective-permute-start(bf16[320,8,8]{0,2,1:T(8,128)(2,1)S(1)} %collective-permute-done.7), channel_id=1, source_target_pairs={{0,30},{2,0},{4,2},{6,4},{8,6},{10,8},{12,10},{14,12},{16,14},{18,... | collective-permute-start | bytes 122888 | tf_op jit(solution)/shard_map/ppermute | solution.py:25
  346.2 0.6 constant_dynamic-update-slice_fusion.10
  346.8 0.6 constant_dynamic-update-slice_fusion.9
  347.4 0.8 collective-permute-done.8
  348.2 5.7 %collective-permute-start.11 = (bf16[320,8,8]{0,2,1:T(8,128)(2,1)S(1)}, bf16[320,8,8]{0,2,1:T(8,128)(2,1)S(1)}, u32[]{:S(2)}, u32[]{:S(2)}) collective-permute-start(bf16[320,8,8]{0,2,1:T(8,128)(2,1)S(1)} %collective-permute-done.9), channel_id=1, source_target_pairs={{0,30},{2,0},{4,2},{6,4},{8,6},{10,8},{12,10},{14,12},{16,14},{18,... | collective-permute-start | bytes 122888 | tf_op jit(solution)/shard_map/ppermute | solution.py:25
  354.0 0.6 constant_dynamic-update-slice_fusion.8
  354.6 0.6 constant_dynamic-update-slice_fusion.7
  355.2 0.7 collective-permute-done.10
  355.9 5.7 %collective-permute-start.13 = (bf16[320,8,8]{0,2,1:T(8,128)(2,1)S(1)}, bf16[320,8,8]{0,2,1:T(8,128)(2,1)S(1)}, u32[]{:S(2)}, u32[]{:S(2)}) collective-permute-start(bf16[320,8,8]{0,2,1:T(8,128)(2,1)S(1)} %collective-permute-done.11), channel_id=1, source_target_pairs={{0,30},{2,0},{4,2},{6,4},{8,6},{10,8},{12,10},{14,12},{16,14},{18,... | collective-permute-start | bytes 122888 | tf_op jit(solution)/shard_map/ppermute | solution.py:25
  361.6 0.6 constant_dynamic-update-slice_fusion.6
  362.3 0.6 constant_dynamic-update-slice_fusion.5
  362.9 0.7 collective-permute-done.12
  363.6 0.6 constant_dynamic-update-slice_fusion.4
  364.2 0.6 constant_dynamic-update-slice_fusion.3
  364.9 6.4 %collective-permute-done.14 = bf16[320,8,8]{0,2,1:T(8,128)(2,1)S(1)} collective-permute-done((bf16[320,8,8]{0,2,1:T(8,128)(2,1)S(1)}, bf16[320,8,8]{0,2,1:T(8,128)(2,1)S(1)}, u32[]{:S(2)}, u32[]{:S(2)}) %collective-permute-start.14) | collective-permute-done | bytes 40992 | tf_op jit(solution)/shard_map/ppermute | solution.py:22
  371.3 0.6 constant_dynamic-update-slice_fusion.2
  371.9 1.3 fusion.12
  373.2 2.5 fusion.8
  375.7 2.7 all-to-all-start
  378.4 1.0 convert_reduce_fusion
  379.5 9.5 %all-to-all-done = bf16[32,32,128]{2,1,0:T(8,128)(2,1)S(1)} async-done(((bf16[32,32,128]{2,1,0:T(8,128)(2,1)}), bf16[32,32,128]{2,1,0:T(8,128)(2,1)S(1)}, u32[]{:S(2)}, u32[]{:S(2)}) %all-to-all-start) | async-done | bytes 262176 | tf_op jit(solution)/shard_map/all_to_all | solution.py:208
  389.2 1.0 maximum_subtract_fusion
  390.2 0.7 slice_bitcast_fusion
  (70 shorter events, 1.3 us)
Async XLA Ops:
  7.2 155.7 %copy-start = (bf16[8192,128]{1,0:T(8,128)(2,1)S(1)}, bf16[8192,128]{1,0:T(8,128)(2,1)}, u32[]{:S(2)}) copy-start(bf16[8192,128]{1,0:T(8,128)(2,1)} %param.16) | copy-start | bytes 6291460
  7.2 97.3 %all-gather.5.cloned.1.call-start = ((), (), s32[]{:S(2)}) async-start(), calls=%async_computation.2 | async-start | bytes 5570560 | tf_op jit(solution)/shard_map/all_gather | solution.py:144
  7.9 159.8 %all-gather.7.cloned.1.call-start = ((), (), s32[]{:S(2)}) async-start(), calls=%async_computation.3 | async-start | bytes 2162688 | tf_op jit(solution)/shard_map/all_gather | solution.py:186
  9.5 247.5 %all-gather.9.cloned.1.call-start = ((), (), s32[]{:S(2)}) async-start(), calls=%async_computation.4 | async-start | bytes 5570560 | tf_op jit(solution)/shard_map/all_gather | solution.py:145
  10.3 304.9 %all-gather.11.cloned.1.call-start = ((), (), s32[]{:S(2)}) async-start(), calls=%async_computation.5 | async-start | bytes 2162688 | tf_op jit(solution)/shard_map/all_gather | solution.py:187
  12.2 96.1 %copy-start.14 = (f32[8192]{0:T(1024)S(1)}, f32[8192]{0:T(1024)}, u32[]{:S(2)}) copy-start(f32[8192]{0:T(1024)} %param.15) | copy-start | bytes 98308
  104.5 4.0 %copy-start.2 = (bf16[320,8192]{1,0:T(8,128)(2,1)S(1)}, bf16[320,8192]{1,0:T(8,128)(2,1)}, u32[]{:S(2)}) copy-start(bf16[320,8192]{1,0:T(8,128)(2,1)} %all-gather.5.cloned.1.call-done) | copy-start | bytes 15728644
  108.5 1.7 copy-start.4
  110.1 7.5 %copy-start.1 = (bf16[320,8192]{1,0:T(8,128)(2,1)}, bf16[320,8192]{1,0:T(8,128)(2,1)S(1)}, u32[]{:S(2)}) copy-start(bf16[320,8192]{1,0:T(8,128)(2,1)S(1)} %fusion.2) | copy-start | bytes 15728644
  110.2 7.4 %copy-start.3 = (bf16[8192,8,8]{0,2,1:T(8,128)(2,1)S(1)}, bf16[8192,8,8]{0,2,1:T(8,128)(2,1)}, u32[]{:S(2)}) copy-start(bf16[8192,8,8]{0,2,1:T(8,128)(2,1)} %param.17) | copy-start | bytes 3145732
  111.9 7.3 %copy-start.5 = (bf16[320,8,128]{0,2,1:T(8,128)(2,1)}, bf16[320,8,128]{0,2,1:T(8,128)(2,1)S(1)}, u32[]{:S(2)}) copy-start(bf16[320,8,128]{0,2,1:T(8,128)(2,1)S(1)} %get-tuple-element.21) | copy-start | bytes 1966084
  111.9 204.6 %collective-permute-start = (bf16[320,8,8]{0,2,1:T(8,128)(2,1)S(1)}, bf16[320,8,8]{0,2,1:T(8,128)(2,1)}, u32[]{:S(2)}, u32[]{:S(2)}) collective-permute-start(bf16[320,8,8]{0,2,1:T(8,128)(2,1)S(1)} %get-tuple-element.22), channel_id=1, source_target_pairs={{0,2},{2,4},{4,6},{6,8},{8,10},{10,12},{12,14},{14,16},{16,18},{18... | collective-permute-start | bytes 122888 | tf_op jit(solution)/shard_map/ppermute | solution.py:22
  113.4 204.6 %collective-permute-start.1 = (bf16[320,8,8]{0,2,1:T(8,128)(2,1)S(1)}, bf16[320,8,8]{0,2,1:T(8,128)(2,1)}, u32[]{:S(2)}, u32[]{:S(2)}) collective-permute-start(bf16[320,8,8]{0,2,1:T(8,128)(2,1)S(1)} %get-tuple-element.22), channel_id=1, source_target_pairs={{0,30},{2,0},{4,2},{6,4},{8,6},{10,8},{12,10},{14,12},{16,14},{18,... | collective-permute-start | bytes 122888 | tf_op jit(solution)/shard_map/ppermute | solution.py:25
  167.7 3.1 copy-start.6
  167.7 3.1 copy-start.7
  169.5 0.8 copy-start.10
  262.8 112.8 %all-to-all-start.1 = ((bf16[32,32,128]{2,1,0:T(8,128)(2,1)}), bf16[32,32,128]{2,1,0:T(8,128)(2,1)}, u32[]{:S(2)}, u32[]{:S(2)}) async-start(bf16[32,32,128]{2,1,0:T(8,128)(2,1)} %bitcast.51), calls=%async_computation.1 | async-start | bytes 524288 | tf_op jit(solution)/shard_map/all_to_all | solution.py:209
  315.2 56.8 %copy-start.11 = (f32[320,320]{0,1:T(8,128)S(1)}, f32[320,320]{0,1:T(8,128)}, u32[]{:S(2)}) copy-start(f32[320,320]{0,1:T(8,128)} %copy-done.10) | copy-start | bytes 1228804
  316.5 8.5 %collective-permute-start.2 = (bf16[320,8,8]{0,2,1:T(8,128)(2,1)}, bf16[320,8,8]{0,2,1:T(8,128)(2,1)S(1)}, u32[]{:S(2)}, u32[]{:S(2)}) collective-permute-start(bf16[320,8,8]{0,2,1:T(8,128)(2,1)} %collective-permute-done), channel_id=1, source_target_pairs={{0,2},{2,4},{4,6},{6,8},{8,10},{10,12},{12,14},{14,16},{16,18},{18... | collective-permute-start | bytes 122888 | tf_op jit(solution)/shard_map/ppermute | solution.py:22
  318.0 7.1 %collective-permute-start.3 = (bf16[320,8,8]{0,2,1:T(8,128)(2,1)}, bf16[320,8,8]{0,2,1:T(8,128)(2,1)S(1)}, u32[]{:S(2)}, u32[]{:S(2)}) collective-permute-start(bf16[320,8,8]{0,2,1:T(8,128)(2,1)} %collective-permute-done.1), channel_id=1, source_target_pairs={{0,30},{2,0},{4,2},{6,4},{8,6},{10,8},{12,10},{14,12},{16,14},{18,... | collective-permute-start | bytes 122888 | tf_op jit(solution)/shard_map/ppermute | solution.py:25
  325.1 7.7 %collective-permute-start.4 = (bf16[320,8,8]{0,2,1:T(8,128)(2,1)S(1)}, bf16[320,8,8]{0,2,1:T(8,128)(2,1)S(1)}, u32[]{:S(2)}, u32[]{:S(2)}) collective-permute-start(bf16[320,8,8]{0,2,1:T(8,128)(2,1)S(1)} %collective-permute-done.2), channel_id=1, source_target_pairs={{0,2},{2,4},{4,6},{6,8},{8,10},{10,12},{12,14},{14,16},{16,18},{18... | collective-permute-start | bytes 122888 | tf_op jit(solution)/shard_map/ppermute | solution.py:22
  325.1 7.7 %collective-permute-start.5 = (bf16[320,8,8]{0,2,1:T(8,128)(2,1)S(1)}, bf16[320,8,8]{0,2,1:T(8,128)(2,1)S(1)}, u32[]{:S(2)}, u32[]{:S(2)}) collective-permute-start(bf16[320,8,8]{0,2,1:T(8,128)(2,1)S(1)} %collective-permute-done.3), channel_id=1, source_target_pairs={{0,30},{2,0},{4,2},{6,4},{8,6},{10,8},{12,10},{14,12},{16,14},{18,... | collective-permute-start | bytes 122888 | tf_op jit(solution)/shard_map/ppermute | solution.py:25
  332.7 7.8 %collective-permute-start.6 = (bf16[320,8,8]{0,2,1:T(8,128)(2,1)S(1)}, bf16[320,8,8]{0,2,1:T(8,128)(2,1)S(1)}, u32[]{:S(2)}, u32[]{:S(2)}) collective-permute-start(bf16[320,8,8]{0,2,1:T(8,128)(2,1)S(1)} %collective-permute-done.4), channel_id=1, source_target_pairs={{0,2},{2,4},{4,6},{6,8},{8,10},{10,12},{12,14},{14,16},{16,18},{18... | collective-permute-start | bytes 122888 | tf_op jit(solution)/shard_map/ppermute | solution.py:22
  332.8 7.8 %collective-permute-start.7 = (bf16[320,8,8]{0,2,1:T(8,128)(2,1)S(1)}, bf16[320,8,8]{0,2,1:T(8,128)(2,1)S(1)}, u32[]{:S(2)}, u32[]{:S(2)}) collective-permute-start(bf16[320,8,8]{0,2,1:T(8,128)(2,1)S(1)} %collective-permute-done.5), channel_id=1, source_target_pairs={{0,30},{2,0},{4,2},{6,4},{8,6},{10,8},{12,10},{14,12},{16,14},{18,... | collective-permute-start | bytes 122888 | tf_op jit(solution)/shard_map/ppermute | solution.py:25
  340.5 7.7 %collective-permute-start.8 = (bf16[320,8,8]{0,2,1:T(8,128)(2,1)S(1)}, bf16[320,8,8]{0,2,1:T(8,128)(2,1)S(1)}, u32[]{:S(2)}, u32[]{:S(2)}) collective-permute-start(bf16[320,8,8]{0,2,1:T(8,128)(2,1)S(1)} %collective-permute-done.6), channel_id=1, source_target_pairs={{0,2},{2,4},{4,6},{6,8},{8,10},{10,12},{12,14},{14,16},{16,18},{18... | collective-permute-start | bytes 122888 | tf_op jit(solution)/shard_map/ppermute | solution.py:22
  340.5 7.7 %collective-permute-start.9 = (bf16[320,8,8]{0,2,1:T(8,128)(2,1)S(1)}, bf16[320,8,8]{0,2,1:T(8,128)(2,1)S(1)}, u32[]{:S(2)}, u32[]{:S(2)}) collective-permute-start(bf16[320,8,8]{0,2,1:T(8,128)(2,1)S(1)} %collective-permute-done.7), channel_id=1, source_target_pairs={{0,30},{2,0},{4,2},{6,4},{8,6},{10,8},{12,10},{14,12},{16,14},{18,... | collective-permute-start | bytes 122888 | tf_op jit(solution)/shard_map/ppermute | solution.py:25
  348.2 7.7 %collective-permute-start.10 = (bf16[320,8,8]{0,2,1:T(8,128)(2,1)S(1)}, bf16[320,8,8]{0,2,1:T(8,128)(2,1)S(1)}, u32[]{:S(2)}, u32[]{:S(2)}) collective-permute-start(bf16[320,8,8]{0,2,1:T(8,128)(2,1)S(1)} %collective-permute-done.8), channel_id=1, source_target_pairs={{0,2},{2,4},{4,6},{6,8},{8,10},{10,12},{12,14},{14,16},{16,18},{18... | collective-permute-start | bytes 122888 | tf_op jit(solution)/shard_map/ppermute | solution.py:22
  348.2 7.7 %collective-permute-start.11 = (bf16[320,8,8]{0,2,1:T(8,128)(2,1)S(1)}, bf16[320,8,8]{0,2,1:T(8,128)(2,1)S(1)}, u32[]{:S(2)}, u32[]{:S(2)}) collective-permute-start(bf16[320,8,8]{0,2,1:T(8,128)(2,1)S(1)} %collective-permute-done.9), channel_id=1, source_target_pairs={{0,30},{2,0},{4,2},{6,4},{8,6},{10,8},{12,10},{14,12},{16,14},{18,... | collective-permute-start | bytes 122888 | tf_op jit(solution)/shard_map/ppermute | solution.py:25
  355.9 7.7 %collective-permute-start.12 = (bf16[320,8,8]{0,2,1:T(8,128)(2,1)S(1)}, bf16[320,8,8]{0,2,1:T(8,128)(2,1)S(1)}, u32[]{:S(2)}, u32[]{:S(2)}) collective-permute-start(bf16[320,8,8]{0,2,1:T(8,128)(2,1)S(1)} %collective-permute-done.10), channel_id=1, source_target_pairs={{0,2},{2,4},{4,6},{6,8},{8,10},{10,12},{12,14},{14,16},{16,18},{18... | collective-permute-start | bytes 122888 | tf_op jit(solution)/shard_map/ppermute | solution.py:22
  355.9 8.3 %collective-permute-start.13 = (bf16[320,8,8]{0,2,1:T(8,128)(2,1)S(1)}, bf16[320,8,8]{0,2,1:T(8,128)(2,1)S(1)}, u32[]{:S(2)}, u32[]{:S(2)}) collective-permute-start(bf16[320,8,8]{0,2,1:T(8,128)(2,1)S(1)} %collective-permute-done.11), channel_id=1, source_target_pairs={{0,30},{2,0},{4,2},{6,4},{8,6},{10,8},{12,10},{14,12},{16,14},{18,... | collective-permute-start | bytes 122888 | tf_op jit(solution)/shard_map/ppermute | solution.py:25
  363.6 7.7 %collective-permute-start.14 = (bf16[320,8,8]{0,2,1:T(8,128)(2,1)S(1)}, bf16[320,8,8]{0,2,1:T(8,128)(2,1)S(1)}, u32[]{:S(2)}, u32[]{:S(2)}) collective-permute-start(bf16[320,8,8]{0,2,1:T(8,128)(2,1)S(1)} %collective-permute-done.12), channel_id=1, source_target_pairs={{0,2},{2,4},{4,6},{6,8},{8,10},{10,12},{12,14},{14,16},{16,18},{18... | collective-permute-start | bytes 122888 | tf_op jit(solution)/shard_map/ppermute | solution.py:22
  375.6 13.6 %copy-start.8 = (f32[32,1024]{1,0:T(8,128)S(1)}, f32[32,1024]{1,0:T(8,128)}, u32[]{:S(2)}) copy-start(f32[32,1024]{1,0:T(8,128)} %param.21) | copy-start | bytes 393220
  375.6 13.6 %copy-start.9 = (f32[32,1024]{1,0:T(8,128)S(1)}, f32[32,1024]{1,0:T(8,128)}, u32[]{:S(2)}) copy-start(f32[32,1024]{1,0:T(8,128)} %param.20) | copy-start | bytes 393220
  375.6 13.6 %copy-start.12 = (f32[2,32,1024]{2,1,0:T(8,128)S(1)}, f32[2,32,1024]{2,1,0:T(8,128)}, u32[]{:S(2)}) copy-start(f32[2,32,1024]{2,1,0:T(8,128)} %param.22) | copy-start | bytes 786436
  375.6 13.6 %copy-start.13 = (f32[2,32,1024]{2,1,0:T(8,128)S(1)}, f32[2,32,1024]{2,1,0:T(8,128)}, u32[]{:S(2)}) copy-start(f32[2,32,1024]{2,1,0:T(8,128)} %param.23) | copy-start | bytes 786436
  375.7 13.3 %all-to-all-start = ((bf16[32,32,128]{2,1,0:T(8,128)(2,1)}), bf16[32,32,128]{2,1,0:T(8,128)(2,1)S(1)}, u32[]{:S(2)}, u32[]{:S(2)}) async-start(bf16[32,32,128]{2,1,0:T(8,128)(2,1)} %bitcast.52), calls=%async_computation | async-start | bytes 524288 | tf_op jit(solution)/shard_map/all_to_all | solution.py:208
Sparse Core Ops, SparseCore 0:
  10.7 93.6 all-gather.4
  107.9 56.6 all-gather.6
  167.4 89.6 all-gather.8
  259.8 55.3 all-gather.10
